TPU v7x, 256 devices: a whole 4x4x8 slice. The times are simulated.
256 devices in a mesh: seq: 16 (over x_lo, z), head: 16 (over y, x_hi, core).
Axes of the slice: x: 4 (x_hi: 2, x_lo: 2; x = x_hi * 2 + x_lo), y: 4, z: 8, core: 2. Of those that a mesh axis runs over, the one named last changes fastest.
Arguments:
- hidden_in: bfloat16 [4096, 7168], P('seq', 'head'), may hold values from -6 to 6
- w_qa: bfloat16 [7168, 1536], P('head'), may hold values from -0.0625 to 0.0625
- w_kva: bfloat16 [7168, 576], P('head'), may hold values from -0.0625 to 0.0625
- q_norm_gain: float32 [1536], replicated, may hold values from 0.5 to 10
- kv_norm_gain: float32 [512], replicated, may hold values from 0.5 to 10
- w_qb: bfloat16 [1536, 12288], P(None, 'head'), may hold values from -0.15625 to 0.15625
- w_uk: bfloat16 [64, 128, 512], P('head'), may hold values from -0.25 to 0.25
- value_up_weight: bfloat16 [64, 512, 128], P('head'), may hold values from -0.25 to 0.25
- positions: int32 [4096], P('seq'), may hold values from 0 to 4095, as said below
Outputs:
- head_values: bfloat16 [4096, 8192], P('seq', 'head')
Inputs may be any that keep to these rules, and one draw needn't show every extreme that they name: A permutation of 0 to 4095 made of aligned runs of 128 rows, each run holding consecutive positions in rising order.
All inputs are finite; a program needn't handle non-finite values.
Results may differ from a plain program's by a relative error of at most 0.025.
The roundings to bfloat16 on the way count: a program that leaves them out, or rounds other values in their place, can miss the bound.
Values may be sent and summed in bfloat16 or wider, within the bound.
A program may use at most 64 MiB of HBM per device.

v0:
```python
import math

import jax
import jax.numpy as jnp
from jax import lax
from jax.sharding import PartitionSpec as P


def frequencies(positions, rope_width):
    exponent = jnp.arange(0, rope_width, 2).astype(jnp.float32) / rope_width
    inverse = 50000.0 ** (-exponent)
    return positions.astype(jnp.float32)[:, None] * inverse[None, :]


def rotate(vector, cosine, sine):
    width = vector.shape[-1] // 2
    first = vector[..., :width]
    second = vector[..., width:]
    return jnp.concatenate([first * cosine - second * sine, second * cosine + first * sine], -1)


def rms_norm(vector, norm_gain):
    return vector * lax.rsqrt(jnp.mean(vector * vector, -1, keepdims=True) + 1e-06) * norm_gain


def body(hidden_in, w_qa, w_kva, q_norm_gain, kv_norm_gain, w_qb, w_uk, value_up_weight, positions):
    count_of_rows = hidden_in.shape[0]
    latent_width = kv_norm_gain.shape[0]
    rope_width = w_kva.shape[1] - latent_width
    head_count = w_uk.shape[0]
    nope_width = w_uk.shape[1]
    angles = frequencies(positions, rope_width)
    cosine = jnp.cos(angles)
    sine = jnp.sin(angles)
    part_q = jnp.dot(hidden_in, w_qa, preferred_element_type=jnp.float32)
    part_kv = jnp.dot(hidden_in, w_kva, preferred_element_type=jnp.float32)
    part_kv = jnp.concatenate(
        [part_kv[:, :latent_width], rotate(part_kv[:, latent_width:], cosine, sine)], 1
    )
    q_low, key_value_latent = lax.psum((part_q, part_kv), "head")
    c_q = rms_norm(q_low, q_norm_gain).astype(jnp.bfloat16)
    keys = jnp.concatenate(
        [
            rms_norm(key_value_latent[:, :latent_width], kv_norm_gain),
            key_value_latent[:, latent_width:],
        ],
        1,
    ).astype(jnp.bfloat16)
    query = jnp.dot(c_q, w_qb, preferred_element_type=jnp.float32).astype(jnp.bfloat16)
    query = query.reshape(count_of_rows, head_count, nope_width + rope_width)
    q_rot = rotate(
        query[..., nope_width:].astype(jnp.float32), cosine[:, None, :], sine[:, None, :]
    ).astype(jnp.bfloat16)
    q_lat = jnp.einsum(
        "thn,hnk->thk", query[..., :nope_width], w_uk, preferred_element_type=jnp.float32
    ).astype(jnp.bfloat16)
    joined = jnp.concatenate([q_lat, q_rot], -1).reshape(
        count_of_rows * head_count, latent_width + rope_width
    )
    query_pos = jnp.repeat(positions, head_count)
    half_rows = count_of_rows // 2
    block_rows = half_rows * head_count
    scale = 1.0 / math.sqrt(nope_width + rope_width)
    query_parts = (joined[:block_rows], joined[block_rows:])
    pos_parts = (query_pos[:block_rows], query_pos[block_rows:])

    def fresh():
        return (
            jnp.full((block_rows,), -1e30, jnp.float32),
            jnp.zeros((block_rows,), jnp.float32),
            jnp.zeros((block_rows, latent_width), jnp.float32),
        )

    carry = (fresh(), fresh())
    key_block = lax.all_gather(keys, "seq", axis=0, tiled=True)
    key_position = lax.all_gather(positions, "seq", axis=0, tiled=True)
    results = []
    for which in range(2):
        queries = query_parts[which]
        qpos = pos_parts[which]
        state = carry[which]
        running_max, total, accum = state
        scores = jnp.dot(queries, key_block.T, preferred_element_type=jnp.float32) * scale
        allowed = key_position[None, :] <= qpos[:, None]
        scores = jnp.where(allowed, scores, -1e30)
        new_max = jnp.maximum(running_max, jnp.max(scores, 1))
        weights = jnp.where(allowed, jnp.exp(scores - new_max[:, None]), 0.0)
        total = jnp.sum(weights, 1)
        accum = jnp.dot(
            weights.astype(jnp.bfloat16),
            key_block[:, :latent_width],
            preferred_element_type=jnp.float32,
        )
        state = (new_max, total, accum)
        results.append(state)
    final = (results[0], results[1])
    latent_output = jnp.concatenate(
        [final[0][2] / final[0][1][:, None], final[1][2] / final[1][1][:, None]], 0
    ).astype(jnp.bfloat16)
    latent_output = latent_output.reshape(count_of_rows, head_count, latent_width)
    value_rows = jnp.einsum(
        "ale,led->ald", latent_output, value_up_weight, preferred_element_type=jnp.float32
    ).astype(jnp.bfloat16)
    return value_rows.reshape(count_of_rows, head_count * value_up_weight.shape[2])


def solution(mesh):
    return jax.shard_map(
        body,
        mesh=mesh,
        in_specs=(
            P("seq", "head"),
            P("head", None),
            P("head", None),
            P(),
            P(),
            P(None, "head"),
            P("head", None, None),
            P("head", None, None),
            P("seq"),
        ),
        out_specs=P("seq", "head"),
        check_vma=False,
    )
```

profile of v0, /device:TPU:0, one launch (start us, length us, event | category | flops | bytes accessed | tf_op | source)
XLA Modules:
  0.0 297.7 jit_solution(2809197218755617969)
XLA Ops:
  6.5 0.0 copy-start
  6.5 0.0 all-reduce.3.cloned.1.call-start
  6.6 0.8 convert_element_type.49
  7.4 1.6 fusion.34
  9.0 3.2 %fusion.33 = f32[256,1536]{1,0:T(8,128)} fusion(bf16[256,448]{0,1:T(8,128)(2,1)} %param.9, bf16[448,1536]{1,0:T(8,128)(2,1)} %param.10), kind=kOutput, calls=%fused_computation.52 | convolution fusion | flops 352321536 | bytes 3178496 | tf_op jit(solution)/shard_map/dot_general | solution.py:35
  12.3 0.2 multiply_cosine_fusion
  12.5 0.9 pad_maximum_fusion.2
  13.3 0.0 all-reduce.3.cloned.1.call-update
  13.4 0.0 all-gather.3.cloned.1.call-start
  13.4 153.3 %all-reduce.3.cloned.1.call-done = (f32[256,576]{0,1:T(8,128)}, f32[256,1536]{1,0:T(8,128)}) async-done(((f32[256,576]{0,1:T(8,128)}, f32[256,1536]{1,0:T(8,128)}), (f32[256,576]{0,1:T(8,128)}, f32[256,1536]{1,0:T(8,128)})) %all-reduce.3.cloned.1.call-update) | async-done | bytes 2162704 | tf_op jit(solution)/shard_map/psum | solution.py:40
  166.7 1.1 multiply_reduce_fusion.1
  167.8 0.8 slice.106
  168.7 0.0 copy-done.3
  168.7 1.2 multiply_convert_fusion.2
  169.9 0.7 pad_maximum_fusion.3
  170.6 0.0 all-gather.3.cloned.1.call-update
  170.7 0.0 copy-done.2
  170.7 0.1 broadcast_in_dim.16
  170.8 0.1 le.32
  170.9 0.1 broadcast_in_dim.13
  171.0 0.1 le.29
  171.1 0.1 copy.30
  171.2 0.1 copy.31
  171.3 32.9 %all-gather = s32[16,1,256]{2,1,0:T(1,128)S(1)} all-gather(s32[1,1,256]{2,1,0:T(1,128)S(1)} %bitcast.27), channel_id=1, replica_groups=mesh['seq'=16,'head'=16] {'seq'}, dimensions={0}, use_global_device_ids=true | all-gather | bytes 17408 | tf_op jit(solution)/shard_map/all_gather | solution.py:76
  204.1 1.6 multiply_reduce_fusion
  205.7 0.0 copy-done
  205.8 0.0 copy-done.1
  205.8 2.2 convolution_convert_fusion.1
  208.0 0.2 copy.27
  208.2 0.2 copy.39
  208.4 0.3 subtract_convert_fusion
  208.7 1.5 fusion.12
  210.2 0.2 pad_maximum_fusion
  210.4 0.1 fusion.31
  210.5 1.4 copy.32
  211.9 2.2 slice.63
  214.1 1.4 copy.33
  215.5 1.5 slice.72
  217.0 49.7 %all-gather.3.cloned.1.call-done = bf16[4096,576]{0,1:T(8,128)(2,1)} async-done(((bf16[256,576]{0,1:T(8,128)(2,1)}), bf16[4096,576]{0,1:T(8,128)(2,1)}) %all-gather.3.cloned.1.call-update) | async-done | bytes 4718608 | tf_op jit(solution)/shard_map/all_gather | solution.py:75
  266.7 6.1 %fusion = (f32[512]{0:T(512)S(1)}, f32[512,4096]{1,0:T(8,128)S(1)}) fusion(s32[4096]{0:T(1024)S(1)} %bitcast.22, s32[512]{0:T(512)S(1)} %le.29, bf16[512,576]{1,0:T(8,128)(2,1)} %slice.63, bf16[4096,576]{0,1:T(8,128)(2,1)} %all-gather.3.cloned.1.call-done), kind=kOutput, calls=%fused_computation.4 | convolution fusion | flops 2424307200 | bytes 13717504 | tf_op jit(solution)/shard_map/dot_general | solution.py:83
  272.9 6.0 %fusion.2 = (f32[512]{0:T(512)S(1)}, f32[512]{0:T(512)S(1)}, f32[512,4096]{1,0:T(8,128)S(1)}) fusion(f32[512,4096]{1,0:T(8,128)S(1)} %get-tuple-element.22, f32[512]{0:T(512)S(1)} %broadcast_maximum_fusion.1, s32[4096]{0:T(1024)S(1)} %bitcast.23, s32[512]{0:T(512)S(1)} %le.29, s32[512]{0:T(512)S(1)} %le.32, bf16[512,576]{1,0:T(8,128)(2,1)S(1)} %slice.72, ...), kind=kOutput, calls=%fused_computation.6 | convolution fusion | flops 2436889600 | bytes 22112256 | tf_op jit(solution)/shard_map/dot_general | solution.py:83
  278.9 2.8 fusion.4
  281.7 2.6 divide_convert_fusion.1
  284.3 2.6 divide_convert_fusion
  286.9 0.1 pad_maximum_fusion.1
  287.0 1.1 convert_element_type.53
  288.2 1.8 convolution_convert_fusion.2
  290.0 0.8 copy.36
  (14 shorter events, 0.1 us)
Async XLA Ops:
  6.5 199.2 %copy-start = (bf16[1536,768]{1,0:T(8,128)(2,1)S(1)}, bf16[1536,768]{1,0:T(8,128)(2,1)}, u32[]{:S(2)}) copy-start(bf16[1536,768]{1,0:T(8,128)(2,1)} %param.14) | copy-start | bytes 7077892
  6.5 164.1 %copy-start.2 = (s32[256]{0:T(256)S(1)}, s32[256]{0:T(256)}, u32[]{:S(2)}) copy-start(s32[256]{0:T(256)} %param.17) | copy-start | bytes 3076
  6.5 162.2 %copy-start.3 = (f32[512]{0:T(512)S(1)}, f32[512]{0:T(512)}, u32[]{:S(2)}) copy-start(f32[512]{0:T(512)} %param.13) | copy-start | bytes 6148
  6.5 199.2 %copy-start.1 = (f32[1536]{0:T(1024)S(1)}, f32[1536]{0:T(1024)}, u32[]{:S(2)}) copy-start(f32[1536]{0:T(1024)} %param.12) | copy-start | bytes 18436
  6.5 160.2 %all-reduce.3.cloned.1.call-start = ((), (), s32[]{:S(2)}) async-start(), calls=%async_computation.1 | async-start | bytes 4325376 | tf_op jit(solution)/shard_map/psum | solution.py:40
  13.4 253.4 %all-gather.3.cloned.1.call-start = ((), (), s32[]{:S(2)}) async-start(), calls=%async_computation | async-start | bytes 5013504 | tf_op jit(solution)/shard_map/all_gather | solution.py:75
  266.7 6.2 %copy-start.4 = (bf16[4096,576]{0,1:T(8,128)(2,1)S(1)}, bf16[4096,576]{0,1:T(8,128)(2,1)}, u32[]{:S(2)}) copy-start(bf16[4096,576]{0,1:T(8,128)(2,1)} %all-gather.3.cloned.1.call-done) | copy-start | bytes 14155780
Sparse Core Ops, SparseCore 0:
  13.5 153.1 all-reduce.2
  170.8 95.8 all-gather.2
where the time goes:
time: 298 us
  waiting for transfers between devices  203 us (68%)
  blocking collectives  32.9 us (11%)
  matrix products  27.8 us (9%)
  between operations  13.6 us (5%)
  local copies, waits for them, and re-layouts  10.4 us (3%)
  other arithmetic  9.91 us (3%)
    psum x1, waiting for transfers between devices, body(): q_low, key_value_latent = lax.psum((part_q, part_kv), 'head')  153 us
    all_gather x1, waiting for transfers between devices, body(): key_block = lax.all_gather(keys, 'seq', axis=0, tiled=True)  49.7 us
    all_gather x1, blocking collectives, body(): key_position = lax.all_gather(positions, 'seq', axis=0, tiled=True)  32.9 us
    dot_general x2, matrix products, body(): jnp.dot(queries, key_block.T, preferred_element_type=jnp.float32) * scale  12.2 us
    slice x5, local copies, waits for them, and re-layouts, body(): query_parts = (joined[:block_rows], joined[block_rows:])  6.58 us
  transfers between devices with their start and end apart: 2, of which 2 were waited for; matrix products, arithmetic and copies ran while one was open for 4% of the time, Pallas kernels for 0%

commit v1 on v0

v1 whole, which is shorter than its diff:
```python
import functools
import math

import jax
import jax.numpy as jnp
import numpy as np
from jax import lax
from jax.experimental import pallas as pl
from jax.experimental.pallas import tpu as pltpu
from jax.sharding import PartitionSpec as P

MESH = pl.DeviceIdType.MESH
F32 = jnp.float32
BF16 = jnp.bfloat16
I16 = jnp.int16
BIG = 2.0**100
KW = 640
QW = 1536 + 128


def place():
    s = lax.axis_index("seq")
    h = lax.axis_index("head")
    return h % 2, ((h // 2) % 2) * 2 + s // 8, h // 4, s % 8


def device(core, x, y, z):
    return ((x % 2) * 8 + z, y * 4 + (x // 2) * 2 + core)


def dot(a, b, over_a=1, over_b=0):
    return lax.dot_general(a, b, (((over_a,), (over_b,)), ((), ())), preferred_element_type=F32)


def encode(values, width):
    rows = values.shape[0]
    top = jnp.maximum(jnp.max(jnp.abs(values), -1, keepdims=True), 2.0**-60)
    level = jnp.ceil(jnp.log2(top) * 512.0)
    digits = jnp.round(values * (jnp.exp2(level * (-1.0 / 512.0)) * 32700.0))
    return digits.astype(jnp.int32).astype(I16), jnp.broadcast_to(level, (rows, width)).astype(jnp.int32).astype(I16)


def decode(digits, level):
    unit = jnp.exp2(level.astype(jnp.int32).astype(F32) * (1.0 / 512.0)) * (1.0 / 32700.0)
    return digits.astype(jnp.int32).astype(F32) * unit


def kernel(
    pos_ref, inv_row_ref, inv_col_ref, qg_ref, kg_ref, hid_hbm, wqa_hbm, wkv_hbm, wqb_hbm, uk_hbm, up_hbm,
    out_ref,
    hid_t, wqa_ref, wkv_ref, wqb_ref, uk_ref, up_ref, hid, uk_t, up_t,
    sx_kv, rx_kv, sx_q, rx_q, own_kv, own_q, st_kv, st_q, rs_kv, rs_q,
    cq_ref, key_ref, ke, vt, qt, s_ref, acc, m, l,
    send, recv, load,
):
    core, x, y, z = place()
    xh, xl = x // 2, x % 2
    j = y * 2 + xh
    p = x * (1 - core) + y * core
    q = y * (1 - core) + x * core
    used = [0]

    loads = []
    for i, (src, dst) in enumerate(
        ((hid_hbm, hid_t), (wkv_hbm, wkv_ref), (wqa_hbm, wqa_ref), (uk_hbm, uk_ref), (up_hbm, up_ref), (wqb_hbm, wqb_ref))
    ):
        loads.append(pltpu.make_async_copy(src, dst, load.at[i]))
        loads[-1].start()

    def copy(src, dst, target):
        at = used[0]
        used[0] += 1
        done = pltpu.make_async_remote_copy(
            src_ref=src, dst_ref=dst, send_sem=send.at[at], recv_sem=recv.at[at],
            device_id=target, device_id_type=MESH,
        )
        done.start()
        return done

    sibling = device(1 - core, x, y, z)
    peers = []
    for d in range(1, 8):
        py, px = (y + d // 2) % 4, (xh + d % 2) % 2
        peers.append((py * 2 + px, device(core, px * 2 + xl, py, z)))
    zs = [device(core, x, y, (z + d) % 8) for d in range(1, 8)]
    sides = [device(core, (x + d) % 4, y, z) for d in (1, 3)]
    barrier = pltpu.get_barrier_semaphore()
    greet = [sibling] + [who for _, who in peers] + zs + sides
    for who in greet:
        pl.semaphore_signal(barrier, inc=1, device_id=who, device_id_type=MESH)

    loads[0].wait()
    rows = hid_t[...].T
    for h in range(16):
        hid[h % 2, 16 * (h // 2) : 16 * (h // 2) + 16] = rows[16 * h : 16 * h + 16]
    other = hid[1 - core]
    mine = hid[core]
    loads[1].wait()
    digits, level = encode(dot(other, wkv_ref[...]), 64)
    sx_kv[:, :, :576] = digits.reshape(8, 16, 576)
    sx_kv[:, :, 576:] = level.reshape(8, 16, 64)
    pl.semaphore_wait(barrier, len(greet))
    c_kv = copy(sx_kv, rx_kv, sibling)
    loads[2].wait()
    digits, level = encode(dot(other, wqa_ref[...]), 128)
    sx_q[:, :, :1536] = digits.reshape(8, 16, 1536)
    sx_q[:, :, 1536:] = level.reshape(8, 16, 128)
    c_q = copy(sx_q, rx_q, sibling)
    own_kv[:, :, 576:] = jnp.zeros((8, 16, 64), F32)
    own_kv[:, :, :576] = dot(mine, wkv_ref[...]).reshape(8, 16, 576)
    own_q[...] = dot(mine, wqa_ref[...]).reshape(8, 16, 1536)

    c_kv.wait()
    low = own_kv[:, :, :576] + decode(rx_kv[:, :, :576], rx_kv[:, :, 576:577])
    own_kv[:, :, :576] = low
    digits, level = encode(low.reshape(128, 576), 64)
    st_kv[:, :, :576] = digits.reshape(8, 16, 576)
    st_kv[:, :, 576:] = level.reshape(8, 16, 64)
    p_kv = [copy(st_kv.at[pj], rs_kv.at[i], who) for i, (pj, who) in enumerate(peers)]
    c_q.wait()
    low = own_q[...] + decode(rx_q[:, :, :1536], rx_q[:, :, 1536:1537])
    own_q[...] = low
    digits, level = encode(low.reshape(128, 1536), 128)
    st_q[:, :, :1536] = digits.reshape(8, 16, 1536)
    st_q[:, :, 1536:] = level.reshape(8, 16, 128)
    p_q = [copy(st_q.at[pj], rs_q.at[i], who) for i, (pj, who) in enumerate(peers)]

    h = j * 2 + core
    base = pos_ref[128 * (h // 8)]
    run = base // 128
    tok = (base + (h % 8) * 16 + lax.broadcasted_iota(jnp.int32, (16, 128), 0)).astype(F32)
    lane = lax.broadcasted_iota(jnp.int32, (16, 128), 1)
    angle = tok * inv_row_ref[...]
    cosine, sine = jnp.cos(angle), jnp.sin(angle)
    tail = jnp.where(lane < 96, jnp.where(run > lane - 64, -BIG, 0.0), 0.0)
    loads[3].wait()
    loads[4].wait()
    for i in range(4):
        uk_t[:, 128 * i : 128 * i + 128] = uk_ref[i].T
        up_t[128 * i : 128 * i + 128, :] = up_ref[i].T
    for c in p_kv:
        c.wait()
    low = own_kv[j]
    parts = [decode(rs_kv[i, :, :576], rs_kv[i, :, 576:577]) for i in range(7)]
    latent = low[:, :512] + sum(part[:, :512] for part in parts)
    latent = latent * lax.rsqrt(jnp.mean(latent * latent, -1, keepdims=True) + 1e-06) * kg_ref[...].reshape(1, 512)
    key_ref[core, p, q, z, :, :512] = latent.astype(BF16)
    rope = sum(part[:, 512:576] for part in parts)
    rope = low[:, 512:] + jnp.concatenate([rope, jnp.zeros((16, 64), F32)], 1)
    swapped = jnp.where(lane < 32, -pltpu.roll(rope, 96, 1), pltpu.roll(rope, 32, 1))
    rope = jnp.where(lane < 64, rope * cosine + swapped * sine, tail)
    key_ref[core, p, q, z, :, 512:] = rope.astype(BF16)
    block = key_ref.at[core, p, q, z]
    p_z = [copy(block, block, who) for who in zs]

    for c in p_q:
        c.wait()
    low = own_q[j]
    for i in range(7):
        low = low + decode(rs_q[i, :, :1536], rs_q[i, :, 1536:1537])
    low = low * lax.rsqrt(jnp.mean(low * low, -1, keepdims=True) + 1e-06) * qg_ref[...].reshape(1, 1536)
    cq_ref[j, core] = low.astype(BF16)
    block = cq_ref.at[j, core]
    p_c = [copy(block, block, who) for _, who in peers]
    for c in p_z:
        c.wait()

    def slot(a, b, lo=0, hi=8):
        return key_ref.at[core, (p + a) % 4, (q + b) % 4, pl.ds(lo, hi - lo)]

    def to(a, b):
        return device(core, (x + a * (1 - core) + b * core) % 4, (y + a * core + b * (1 - core)) % 4, z)

    def ring(a, b, da, db):
        return [copy(slot(a, b), slot(a, b), to(da, db)), copy(slot(a, b), slot(a, b), to(3 * da, 3 * db))]

    def onward(pair, a, b, da, db):
        for c in pair:
            c.wait()
        left, right = slot(a + 3 * da, b + 3 * db, 0, 4), slot(a + da, b + db, 4, 8)
        return [copy(left, left, to(da, db)), copy(right, right, to(3 * da, 3 * db))]

    def share(a):
        line = key_ref.at[core, (p + a) % 4]
        return copy(line, line, sibling)

    first = ring(0, 0, 1, 0)
    lines = {0: ring(0, 0, 0, 1)}
    first = onward(first, 0, 0, 1, 0)
    lines[1] = ring(1, 0, 0, 1)
    lines[3] = ring(3, 0, 0, 1)
    lines[0] = onward(lines[0], 0, 0, 0, 1)
    for c in p_c:
        c.wait()
    mate = cq_ref.at[:, pl.ds(core, 1)]
    c_c = copy(mate, mate, sibling)
    for c in first:
        c.wait()
    lines[2] = ring(2, 0, 0, 1)

    def finish(a):
        for c in lines[a]:
            c.wait()
        return share(a)

    sp = y * (1 - core) + x * core

    def chunk(n):
        a = (0, 1, 3, 2)[n % 4]
        return (core, (p + a) % 4) if n < 4 else (1 - core, (sp + a) % 4)

    def expand(n):
        keys = key_ref[chunk(n)].reshape(512, KW)[:, :512]
        ke[n] = dot(keys, uk_t[...]).astype(BF16)
        vt[n] = dot(up_t[...], keys, 1, 1).astype(BF16)

    scale = math.log2(math.e) / math.sqrt(192)
    token = lax.broadcasted_iota(jnp.int32, (16, 256), 1)
    row = lax.broadcasted_iota(jnp.int32, (16, 256), 0)

    def attend(n):
        k, line = chunk(n)
        tails = key_ref[k, line].reshape(512, KW)[:, 512:]
        for i in range(4):
            s_ref[i] = dot(jnp.concatenate([ke[n, :, 128 * i : 128 * i + 128], tails], 1), qt[i])
        for b in range(4):
            kx = line * (1 - k) + b * k
            ky = b * (1 - k) + line * k
            key_token = (ky * 4 + (kx // 2) * 2 + k) * 16 + row
            hidden = (key_token > token) & (key_token // 128 == token // 128) & (kx % 2 == xl)
            strip = pl.ds(pl.multiple_of(b * 128 + z * 16, 16), 16)
            for i in range(4):
                s_ref[i, strip] = jnp.where(hidden, -BIG, s_ref[i, strip])
        for i in range(4):
            s = s_ref[i] * scale
            before = m[i]
            now = jnp.maximum(before, jnp.max(s, 0, keepdims=True))
            w = jnp.exp2(s - now)
            fade = jnp.exp2(before - now)
            l[i] = l[i] * fade + jnp.sum(w, 0, keepdims=True)
            m[i] = now
            acc[i] = acc[i] * fade + dot(vt[n, 128 * i : 128 * i + 128], w.astype(BF16))

    s_lines = {0: finish(0)}
    expand(0)
    m[...] = jnp.full(m.shape, -4 * BIG, F32)
    l[...] = jnp.zeros(l.shape, F32)
    acc[...] = jnp.zeros(acc.shape, F32)
    wide = lax.broadcasted_iota(jnp.int32, (32, 256), 1)
    base = jnp.where(wide < 128, pos_ref[0], pos_ref[128])
    angle = (base + wide % 128).astype(F32) * inv_col_ref[...]
    cosine, sine = jnp.cos(angle), jnp.sin(angle)
    runs = jnp.where(base // 128 == lax.broadcasted_iota(jnp.int32, (32, 256), 0), 1.0, 0.0).astype(BF16)
    loads[5].wait()
    c_c.wait()
    q_t = dot(cq_ref[...].reshape(256, 1536), wqb_ref[...]).astype(BF16).T
    for i in range(4):
        qt[i, :128] = q_t[192 * i : 192 * i + 128]
        a = q_t[192 * i + 128 : 192 * i + 160].astype(F32)
        b = q_t[192 * i + 160 : 192 * i + 192].astype(F32)
        qt[i, 128:160] = (a * cosine - b * sine).astype(BF16)
        qt[i, 160:192] = (b * cosine + a * sine).astype(BF16)
        qt[i, 192:224] = runs
        qt[i, 224:] = jnp.zeros((32, 256), BF16)
    s_lines[0].wait()
    expand(4)
    for a in (1, 3):
        lines[a] = onward(lines[a], a, 0, 0, 1)
    attend(0)
    attend(4)
    for a in (1, 3):
        s_lines[a] = finish(a)
    lines[2] = onward(lines[2], 2, 0, 0, 1)
    for n in (1, 2):
        expand(n)
        attend(n)
    s_lines[2] = finish(2)
    for n, a in ((5, 1), (6, 3)):
        s_lines[a].wait()
        expand(n)
        attend(n)
    expand(3)
    attend(3)
    s_lines[2].wait()
    expand(7)
    attend(7)
    for i in range(4):
        out_ref[:, 128 * i : 128 * i + 128] = (acc[i] / l[i]).T.astype(BF16)


def body(hidden_in, w_qa, w_kva, q_norm_gain, kv_norm_gain, w_qb, w_uk, value_up_weight, positions):
    inverse = 50000.0 ** (-np.arange(0, 64, 2) / 64)
    inv_row = np.zeros((1, 128), np.float32)
    inv_row[0, :32] = inverse
    inv_row[0, 32:64] = inverse
    inv_col = np.repeat(inverse.astype(np.float32)[:, None], 256, 1)
    vmem = pl.BlockSpec(memory_space=pltpu.VMEM)
    smem = pl.BlockSpec(memory_space=pltpu.SMEM)
    any_space = pl.BlockSpec(memory_space=pl.ANY)
    copies = 64
    return pl.pallas_call(
        kernel,
        name="attention",
        out_shape=jax.ShapeDtypeStruct((256, 512), BF16),
        in_specs=[smem] + [vmem] * 4 + [any_space] * 6,
        out_specs=vmem,
        scratch_shapes=[
            pltpu.VMEM((448, 256), BF16), pltpu.VMEM((448, 1536), BF16), pltpu.VMEM((448, 576), BF16),
            pltpu.VMEM((1536, 768), BF16), pltpu.VMEM((4, 128, 512), BF16), pltpu.VMEM((4, 512, 128), BF16),
            pltpu.VMEM((2, 128, 448), BF16), pltpu.VMEM((512, 512), BF16), pltpu.VMEM((512, 512), BF16),
            pltpu.VMEM((8, 16, KW), I16), pltpu.VMEM((8, 16, KW), I16),
            pltpu.VMEM((8, 16, QW), I16), pltpu.VMEM((8, 16, QW), I16),
            pltpu.VMEM((8, 16, KW), F32), pltpu.VMEM((8, 16, 1536), F32),
            pltpu.VMEM((8, 16, KW), I16), pltpu.VMEM((8, 16, QW), I16),
            pltpu.VMEM((7, 16, KW), I16), pltpu.VMEM((7, 16, QW), I16),
            pltpu.VMEM((8, 2, 16, 1536), BF16), pltpu.VMEM((2, 4, 4, 8, 16, KW), BF16),
            pltpu.VMEM((8, 512, 512), BF16), pltpu.VMEM((8, 512, 512), BF16),
            pltpu.VMEM((4, 256, 256), BF16), pltpu.VMEM((4, 512, 256), F32),
            pltpu.VMEM((4, 128, 256), F32), pltpu.VMEM((4, 1, 256), F32), pltpu.VMEM((4, 1, 256), F32),
            pltpu.SemaphoreType.DMA((copies,)), pltpu.SemaphoreType.DMA((copies,)), pltpu.SemaphoreType.DMA((6,)),
        ],
        compiler_params=pltpu.CompilerParams(
            collective_id=0, has_side_effects=True, vmem_limit_bytes=60 * 2**20
        ),
    )(
        positions, jnp.asarray(inv_row), jnp.asarray(inv_col), q_norm_gain, kv_norm_gain,
        hidden_in.T, w_qa, w_kva, w_qb, w_uk, value_up_weight,
    )


def solution(mesh):
    return jax.shard_map(
        body,
        mesh=mesh,
        in_specs=(
            P("seq", "head"), P("head", None), P("head", None), P(), P(), P(None, "head"),
            P("head", None, None), P("head", None, None), P("seq"),
        ),
        out_specs=P("seq", "head"),
        check_vma=False,
    )
```

time: 298 us -> 61.5 us (0.21)
  the two profiles are of different devices: /device:TPU:0 before, /device:TPU:1 now
where the time goes in v1:
time: 61.5 us; the launch traced here: 61.4 us
  Pallas kernels  59.7 us (97%)
  local copies, waits for them, and re-layouts  1.67 us (3%)
    pallas_call x1, Pallas kernels, body(): pl.pallas_call(kernel, name='attention', out_shape=jax.ShapeDtypeStruct((...  59.7 us
    unnamed x1, local copies, waits for them, and re-layouts  1.67 us

profile of v1, /device:TPU:1, one launch (start us, length us, event | category | flops | bytes accessed | tf_op | source)
XLA Modules:
  0.0 61.4 jit_solution(11884135562988493189)
XLA Ops:
  0.0 59.7 %attention.1 = bf16[256,512]{1,0:T(8,128)(2,1)} custom-call(s32[256]{0:T(256)} %pos_ref.1, f32[1,128]{1,0:T(1,128)} %constant.4.clone.inv_row_ref, f32[32,256]{1,0:T(8,128)} %constant.5.clone.inv_col_ref, f32[1536]{0:T(1024)} %qg_ref.1, f32[512]{0:T(512)} %kg_ref.1, bf16[448,256]{1,0:T(8,128)(2,1)} %bitcast.1, bf16[448,1536]{1,0:T(8,128)(2,1)} %wqa_hbm.1, ...), custom_call_target="tpu_custom_call" | custom-call | tf_op jit(solution)/shard_map/attention/pallas_call | solution.py:301
  59.7 1.7 %copy.13 = bf16[256,512]{1,0:T(8,128)(2,1)} copy(bf16[256,512]{1,0:T(8,128)(2,1)} %attention.1) | data formatting | bytes 524288

commit v2 on v1

--- a/solution.py
+++ b/solution.py
@@ -50,7 +50,7 @@
     out_ref,
     hid_t, wqa_ref, wkv_ref, wqb_ref, uk_ref, up_ref, hid, uk_t, up_t,
     sx_kv, rx_kv, sx_q, rx_q, own_kv, own_q, st_kv, st_q, rs_kv, rs_q,
-    cq_ref, key_ref, ke, vt, qt, s_ref, acc, m, l,
+    cq_ref, near_ref, far_ref, ke, vt, qt, s_ref, acc, m, l,
     send, recv, load,
 ):
     core, x, y, z = place()
@@ -82,10 +82,10 @@
     for d in range(1, 8):
         py, px = (y + d // 2) % 4, (xh + d % 2) % 2
         peers.append((py * 2 + px, device(core, px * 2 + xl, py, z)))
-    zs = [device(core, x, y, (z + d) % 8) for d in range(1, 8)]
-    sides = [device(core, (x + d) % 4, y, z) for d in (1, 3)]
+    zs = [device(core, x, y, (z + d) % 8) for d in range(8)]
+    plane = [device(core, (x + d % 4) % 4, (y + d // 4) % 4, z) for d in range(1, 16)]
     barrier = pltpu.get_barrier_semaphore()
-    greet = [sibling] + [who for _, who in peers] + zs + sides
+    greet = [sibling] + zs[1:] + plane
     for who in greet:
         pl.semaphore_signal(barrier, inc=1, device_id=who, device_id_type=MESH)
 
@@ -144,14 +144,15 @@
     parts = [decode(rs_kv[i, :, :576], rs_kv[i, :, 576:577]) for i in range(7)]
     latent = low[:, :512] + sum(part[:, :512] for part in parts)
     latent = latent * lax.rsqrt(jnp.mean(latent * latent, -1, keepdims=True) + 1e-06) * kg_ref[...].reshape(1, 512)
-    key_ref[core, p, q, z, :, :512] = latent.astype(BF16)
+    near_ref[core, 0, p, q, :, :512] = latent.astype(BF16)
     rope = sum(part[:, 512:576] for part in parts)
     rope = low[:, 512:] + jnp.concatenate([rope, jnp.zeros((16, 64), F32)], 1)
     swapped = jnp.where(lane < 32, -pltpu.roll(rope, 96, 1), pltpu.roll(rope, 32, 1))
     rope = jnp.where(lane < 64, rope * cosine + swapped * sine, tail)
-    key_ref[core, p, q, z, :, 512:] = rope.astype(BF16)
-    block = key_ref.at[core, p, q, z]
-    p_z = [copy(block, block, who) for who in zs]
+    near_ref[core, 0, p, q, :, 512:] = rope.astype(BF16)
+    block = near_ref.at[core, 0, p, q]
+    p_z = [copy(block, far_ref.at[core, p, q, d - 2], zs[d]) for d in range(2, 7)]
+    p_p = [copy(block, block, who) for who in plane]
 
     for c in p_q:
         c.wait()
@@ -162,87 +163,83 @@
     cq_ref[j, core] = low.astype(BF16)
     block = cq_ref.at[j, core]
     p_c = [copy(block, block, who) for _, who in peers]
+
+    def share(part):
+        return copy(part, part, sibling)
+
+    for c in p_p:
+        c.wait()
+    mine = near_ref.at[core, 0]
+    beside = [copy(mine, near_ref.at[core, 1], zs[1]), copy(mine, near_ref.at[core, 2], zs[7])]
+    s_near = [share(mine)]
+
     for c in p_z:
         c.wait()
 
-    def slot(a, b, lo=0, hi=8):
-        return key_ref.at[core, (p + a) % 4, (q + b) % 4, pl.ds(lo, hi - lo)]
-
-    def to(a, b):
-        return device(core, (x + a * (1 - core) + b * core) % 4, (y + a * core + b * (1 - core)) % 4, z)
-
-    def ring(a, b, da, db):
-        return [copy(slot(a, b), slot(a, b), to(da, db)), copy(slot(a, b), slot(a, b), to(3 * da, 3 * db))]
-
-    def onward(pair, a, b, da, db):
-        for c in pair:
-            c.wait()
-        left, right = slot(a + 3 * da, b + 3 * db, 0, 4), slot(a + da, b + db, 4, 8)
-        return [copy(left, left, to(da, db)), copy(right, right, to(3 * da, 3 * db))]
-
-    def share(a):
-        line = key_ref.at[core, (p + a) % 4]
-        return copy(line, line, sibling)
-
-    first = ring(0, 0, 1, 0)
-    lines = {0: ring(0, 0, 0, 1)}
-    first = onward(first, 0, 0, 1, 0)
-    lines[1] = ring(1, 0, 0, 1)
-    lines[3] = ring(3, 0, 0, 1)
-    lines[0] = onward(lines[0], 0, 0, 0, 1)
-    for c in p_c:
-        c.wait()
-    mate = cq_ref.at[:, pl.ds(core, 1)]
-    c_c = copy(mate, mate, sibling)
-    for c in first:
-        c.wait()
-    lines[2] = ring(2, 0, 0, 1)
+    def spread(a, steps):
+        part = far_ref.at[core, (p + a) % 4, q]
+        return [
+            copy(part, part, device(
+                core, (x + da * (1 - core) + db * core) % 4, (y + da * core + db * (1 - core)) % 4, z,
+            ))
+            for da, db in steps
+        ]
+
+    across = ((0, 1), (0, 3), (0, 2))
+    first = spread(0, ((1, 0), (3, 0), (2, 0)))
+    lines = {0: spread(0, across)}
+    s_lines = {}
 
     def finish(a):
         for c in lines[a]:
             c.wait()
-        return share(a)
+        s_lines[a] = share(far_ref.at[core, (p + a) % 4])
 
     sp = y * (1 - core) + x * core
-
-    def chunk(n):
-        a = (0, 1, 3, 2)[n % 4]
-        return (core, (p + a) % 4) if n < 4 else (1 - core, (sp + a) % 4)
-
-    def expand(n):
-        keys = key_ref[chunk(n)].reshape(512, KW)[:, :512]
-        ke[n] = dot(keys, uk_t[...]).astype(BF16)
-        vt[n] = dot(up_t[...], keys, 1, 1).astype(BF16)
-
     scale = math.log2(math.e) / math.sqrt(192)
-    token = lax.broadcasted_iota(jnp.int32, (16, 256), 1)
-    row = lax.broadcasted_iota(jnp.int32, (16, 256), 0)
-
-    def attend(n):
-        k, line = chunk(n)
-        tails = key_ref[k, line].reshape(512, KW)[:, 512:]
+
+    def near_keys(r, cols):
+        return near_ref[:, r, :, :, :, cols].reshape(512, -1)
+
+    def far_keys(a, cols):
+        return jnp.concatenate([
+            far_ref[core, (p + a) % 4, :, :, :, cols].reshape(320, -1),
+            far_ref[1 - core, (sp + a) % 4, :, :, :, cols].reshape(320, -1),
+        ], 0)
+
+    def expand(n, keys, which):
+        keys = keys(which, slice(0, 512))
+        count = keys.shape[0]
+        ke[n, :count] = dot(keys, uk_t[...]).astype(BF16)
+        vt[n, :, :count] = dot(up_t[...], keys, 1, 1).astype(BF16)
+
+    def attend(n, keys, which, diagonal=False):
+        tails = keys(which, slice(512, KW))
+        count = tails.shape[0]
         for i in range(4):
-            s_ref[i] = dot(jnp.concatenate([ke[n, :, 128 * i : 128 * i + 128], tails], 1), qt[i])
-        for b in range(4):
-            kx = line * (1 - k) + b * k
-            ky = b * (1 - k) + line * k
-            key_token = (ky * 4 + (kx // 2) * 2 + k) * 16 + row
-            hidden = (key_token > token) & (key_token // 128 == token // 128) & (kx % 2 == xl)
-            strip = pl.ds(pl.multiple_of(b * 128 + z * 16, 16), 16)
-            for i in range(4):
-                s_ref[i, strip] = jnp.where(hidden, -BIG, s_ref[i, strip])
+            s_ref[i, :count] = dot(jnp.concatenate([ke[n, :count, 128 * i : 128 * i + 128], tails], 1), qt[i])
+        if diagonal:
+            token = lax.broadcasted_iota(jnp.int32, (16, 256), 1)
+            row = lax.broadcasted_iota(jnp.int32, (16, 256), 0)
+            for k in range(2):
+                for ky in range(4):
+                    for half in range(2):
+                        at = (ky * 4 + xl + 2 * half) if k else ((xl + 2 * half) * 4 + ky)
+                        strip = pl.ds(pl.multiple_of(k * 256 + at * 16, 16), 16)
+                        key_token = (ky * 4 + half * 2 + k) * 16 + row
+                        hidden = (key_token > token) & (key_token // 128 == token // 128)
+                        for i in range(4):
+                            s_ref[i, strip] = jnp.where(hidden, -BIG, s_ref[i, strip])
         for i in range(4):
-            s = s_ref[i] * scale
+            s = s_ref[i, :count] * scale
             before = m[i]
             now = jnp.maximum(before, jnp.max(s, 0, keepdims=True))
             w = jnp.exp2(s - now)
             fade = jnp.exp2(before - now)
             l[i] = l[i] * fade + jnp.sum(w, 0, keepdims=True)
             m[i] = now
-            acc[i] = acc[i] * fade + dot(vt[n, 128 * i : 128 * i + 128], w.astype(BF16))
-
-    s_lines = {0: finish(0)}
-    expand(0)
+            acc[i] = acc[i] * fade + dot(vt[n, 128 * i : 128 * i + 128, :count], w.astype(BF16))
+
     m[...] = jnp.full(m.shape, -4 * BIG, F32)
     l[...] = jnp.zeros(l.shape, F32)
     acc[...] = jnp.zeros(acc.shape, F32)
@@ -251,6 +248,15 @@
     angle = (base + wide % 128).astype(F32) * inv_col_ref[...]
     cosine, sine = jnp.cos(angle), jnp.sin(angle)
     runs = jnp.where(base // 128 == lax.broadcasted_iota(jnp.int32, (32, 256), 0), 1.0, 0.0).astype(BF16)
+    s_near[0].wait()
+    expand(0, near_keys, 0)
+    for c in p_c:
+        c.wait()
+    mate = cq_ref.at[:, pl.ds(core, 1)]
+    c_c = share(mate)
+    for c, a in zip(first, (3, 1, 2)):
+        c.wait()
+        lines[a] = spread(a, across)
     loads[5].wait()
     c_c.wait()
     q_t = dot(cq_ref[...].reshape(256, 1536), wqb_ref[...]).astype(BF16).T
@@ -262,28 +268,32 @@
         qt[i, 160:192] = (b * cosine + a * sine).astype(BF16)
         qt[i, 192:224] = runs
         qt[i, 224:] = jnp.zeros((32, 256), BF16)
+    finish(0)
+    attend(0, near_keys, 0, True)
+    for r in (1, 2):
+        beside[r - 1].wait()
+        s_near.append(share(near_ref.at[core, r]))
     s_lines[0].wait()
-    expand(4)
-    for a in (1, 3):
-        lines[a] = onward(lines[a], a, 0, 0, 1)
-    attend(0)
-    attend(4)
-    for a in (1, 3):
-        s_lines[a] = finish(a)
-    lines[2] = onward(lines[2], 2, 0, 0, 1)
-    for n in (1, 2):
-        expand(n)
-        attend(n)
-    s_lines[2] = finish(2)
-    for n, a in ((5, 1), (6, 3)):
-        s_lines[a].wait()
-        expand(n)
-        attend(n)
-    expand(3)
-    attend(3)
+    expand(3, far_keys, 0)
+    finish(3)
+    attend(3, far_keys, 0)
+    s_near[1].wait()
+    expand(1, near_keys, 1)
+    attend(1, near_keys, 1)
+    finish(1)
+    s_lines[3].wait()
+    expand(4, far_keys, 3)
+    attend(4, far_keys, 3)
+    s_near[2].wait()
+    expand(2, near_keys, 2)
+    attend(2, near_keys, 2)
+    finish(2)
+    s_lines[1].wait()
+    expand(5, far_keys, 1)
+    attend(5, far_keys, 1)
     s_lines[2].wait()
-    expand(7)
-    attend(7)
+    expand(6, far_keys, 2)
+    attend(6, far_keys, 2)
     for i in range(4):
         out_ref[:, 128 * i : 128 * i + 128] = (acc[i] / l[i]).T.astype(BF16)
 
@@ -297,7 +307,7 @@
     vmem = pl.BlockSpec(memory_space=pltpu.VMEM)
     smem = pl.BlockSpec(memory_space=pltpu.SMEM)
     any_space = pl.BlockSpec(memory_space=pl.ANY)
-    copies = 64
+    copies = 80
     return pl.pallas_call(
         kernel,
         name="attention",
@@ -313,9 +323,10 @@
             pltpu.VMEM((8, 16, KW), F32), pltpu.VMEM((8, 16, 1536), F32),
             pltpu.VMEM((8, 16, KW), I16), pltpu.VMEM((8, 16, QW), I16),
             pltpu.VMEM((7, 16, KW), I16), pltpu.VMEM((7, 16, QW), I16),
-            pltpu.VMEM((8, 2, 16, 1536), BF16), pltpu.VMEM((2, 4, 4, 8, 16, KW), BF16),
-            pltpu.VMEM((8, 512, 512), BF16), pltpu.VMEM((8, 512, 512), BF16),
-            pltpu.VMEM((4, 256, 256), BF16), pltpu.VMEM((4, 512, 256), F32),
+            pltpu.VMEM((8, 2, 16, 1536), BF16), pltpu.VMEM((2, 3, 4, 4, 16, KW), BF16),
+            pltpu.VMEM((2, 4, 4, 5, 16, KW), BF16),
+            pltpu.VMEM((7, 640, 512), BF16), pltpu.VMEM((7, 512, 640), BF16),
+            pltpu.VMEM((4, 256, 256), BF16), pltpu.VMEM((4, 640, 256), F32),
             pltpu.VMEM((4, 128, 256), F32), pltpu.VMEM((4, 1, 256), F32), pltpu.VMEM((4, 1, 256), F32),
             pltpu.SemaphoreType.DMA((copies,)), pltpu.SemaphoreType.DMA((copies,)), pltpu.SemaphoreType.DMA((6,)),
         ],

time: 61.5 us -> 52.1 us (0.85)
  Pallas kernels: 59.7 us -> 50.2 us
    pallas_call x1, Pallas kernels: 59.7 us -> 50.2 us  [body(): pl.pallas_call(kernel, name='attention', out_shape=jax.ShapeDtypeStruct((...]
where the time goes in v2:
time: 52.1 us; the launch traced here: 51.9 us
  Pallas kernels  50.2 us (96%)
  local copies, waits for them, and re-layouts  1.67 us (3%)
    pallas_call x1, Pallas kernels, body(): pl.pallas_call(kernel, name='attention', out_shape=jax.ShapeDtypeStruct((...  50.2 us
    unnamed x1, local copies, waits for them, and re-layouts  1.67 us

profile of v2, /device:TPU:1, one launch (start us, length us, event | category | flops | bytes accessed | tf_op | source)
XLA Modules:
  0.0 51.9 jit_solution(8050023654294811214)
XLA Ops:
  0.0 50.2 %attention.1 = bf16[256,512]{1,0:T(8,128)(2,1)} custom-call(s32[256]{0:T(256)} %pos_ref.1, f32[1,128]{1,0:T(1,128)} %constant.4.clone.inv_row_ref, f32[32,256]{1,0:T(8,128)} %constant.5.clone.inv_col_ref, f32[1536]{0:T(1024)} %qg_ref.1, f32[512]{0:T(512)} %kg_ref.1, bf16[448,256]{1,0:T(8,128)(2,1)} %bitcast.1, bf16[448,1536]{1,0:T(8,128)(2,1)} %wqa_hbm.1, ...), custom_call_target="tpu_custom_call" | custom-call | tf_op jit(solution)/shard_map/attention/pallas_call | solution.py:311
  50.2 1.7 %copy.13 = bf16[256,512]{1,0:T(8,128)(2,1)} copy(bf16[256,512]{1,0:T(8,128)(2,1)} %attention.1) | data formatting | bytes 524288

commit v3 on v2

--- a/solution.py
+++ b/solution.py
@@ -46,9 +46,9 @@
 
 
 def kernel(
-    pos_ref, inv_row_ref, inv_col_ref, qg_ref, kg_ref, hid_hbm, wqa_hbm, wkv_hbm, wqb_hbm, uk_hbm, up_hbm,
+    pos_ref, row_hbm, col_hbm, qg_hbm, kg_hbm, hid_hbm, wqa_hbm, wkv_hbm, wqb_hbm, uk_hbm, up_hbm,
     out_ref,
-    hid_t, wqa_ref, wkv_ref, wqb_ref, uk_ref, up_ref, hid, uk_t, up_t,
+    inv_row_ref, inv_col_ref, qg_ref, kg_ref, hid_t, wqa_ref, wkv_ref, wqb_ref, uk_ref, up_ref, hid, uk_t, up_t,
     sx_kv, rx_kv, sx_q, rx_q, own_kv, own_q, st_kv, st_q, rs_kv, rs_q,
     cq_ref, near_ref, far_ref, ke, vt, qt, s_ref, acc, m, l,
     send, recv, load,
@@ -61,11 +61,13 @@
     used = [0]
 
     loads = []
-    for i, (src, dst) in enumerate(
-        ((hid_hbm, hid_t), (wkv_hbm, wkv_ref), (wqa_hbm, wqa_ref), (uk_hbm, uk_ref), (up_hbm, up_ref), (wqb_hbm, wqb_ref))
-    ):
-        loads.append(pltpu.make_async_copy(src, dst, load.at[i]))
-        loads[-1].start()
+
+    def fetch(*pairs):
+        for src, dst in pairs:
+            loads.append(pltpu.make_async_copy(src, dst, load.at[len(loads)]))
+            loads[-1].start()
+
+    fetch((hid_hbm, hid_t), (wkv_hbm, wkv_ref))
 
     def copy(src, dst, target):
         at = used[0]
@@ -79,11 +81,12 @@
 
     sibling = device(1 - core, x, y, z)
     peers = []
-    for d in range(1, 8):
-        py, px = (y + d // 2) % 4, (xh + d % 2) % 2
+    for dy, dx in ((2, 1), (1, 1), (3, 1), (2, 0), (0, 1), (1, 0), (3, 0)):
+        py, px = (y + dy) % 4, (xh + dx) % 2
         peers.append((py * 2 + px, device(core, px * 2 + xl, py, z)))
     zs = [device(core, x, y, (z + d) % 8) for d in range(8)]
-    plane = [device(core, (x + d % 4) % 4, (y + d // 4) % 4, z) for d in range(1, 16)]
+    order = (10, 9, 11, 6, 14, 2, 8, 5, 7, 13, 15, 1, 3, 4, 12)
+    plane = [device(core, (x + d % 4) % 4, (y + d // 4) % 4, z) for d in order]
     barrier = pltpu.get_barrier_semaphore()
     greet = [sibling] + zs[1:] + plane
     for who in greet:
@@ -96,6 +99,7 @@
     other = hid[1 - core]
     mine = hid[core]
     loads[1].wait()
+    fetch((wqa_hbm, wqa_ref))
     digits, level = encode(dot(other, wkv_ref[...]), 64)
     sx_kv[:, :, :576] = digits.reshape(8, 16, 576)
     sx_kv[:, :, 576:] = level.reshape(8, 16, 64)
@@ -106,35 +110,38 @@
     sx_q[:, :, :1536] = digits.reshape(8, 16, 1536)
     sx_q[:, :, 1536:] = level.reshape(8, 16, 128)
     c_q = copy(sx_q, rx_q, sibling)
+    fetch((uk_hbm, uk_ref), (up_hbm, up_ref), (qg_hbm, qg_ref), (kg_hbm, kg_ref), (row_hbm, inv_row_ref), (col_hbm, inv_col_ref))
+    low = dot(mine, wkv_ref[...]).reshape(8, 16, 576)
+
+    c_kv.wait()
+    low = low + decode(rx_kv[:, :, :576], rx_kv[:, :, 576:577])
+    own_kv[:, :, :576] = low
     own_kv[:, :, 576:] = jnp.zeros((8, 16, 64), F32)
-    own_kv[:, :, :576] = dot(mine, wkv_ref[...]).reshape(8, 16, 576)
-    own_q[...] = dot(mine, wqa_ref[...]).reshape(8, 16, 1536)
-
-    c_kv.wait()
-    low = own_kv[:, :, :576] + decode(rx_kv[:, :, :576], rx_kv[:, :, 576:577])
-    own_kv[:, :, :576] = low
     digits, level = encode(low.reshape(128, 576), 64)
     st_kv[:, :, :576] = digits.reshape(8, 16, 576)
     st_kv[:, :, 576:] = level.reshape(8, 16, 64)
     p_kv = [copy(st_kv.at[pj], rs_kv.at[i], who) for i, (pj, who) in enumerate(peers)]
+    low = dot(mine, wqa_ref[...]).reshape(8, 16, 1536)
     c_q.wait()
-    low = own_q[...] + decode(rx_q[:, :, :1536], rx_q[:, :, 1536:1537])
+    low = low + decode(rx_q[:, :, :1536], rx_q[:, :, 1536:1537])
     own_q[...] = low
     digits, level = encode(low.reshape(128, 1536), 128)
     st_q[:, :, :1536] = digits.reshape(8, 16, 1536)
     st_q[:, :, 1536:] = level.reshape(8, 16, 128)
     p_q = [copy(st_q.at[pj], rs_q.at[i], who) for i, (pj, who) in enumerate(peers)]
 
+    fetch((wqb_hbm, wqb_ref))
+
     h = j * 2 + core
     base = pos_ref[128 * (h // 8)]
     run = base // 128
     tok = (base + (h % 8) * 16 + lax.broadcasted_iota(jnp.int32, (16, 128), 0)).astype(F32)
     lane = lax.broadcasted_iota(jnp.int32, (16, 128), 1)
+    for i in range(3, 9):
+        loads[i].wait()
     angle = tok * inv_row_ref[...]
     cosine, sine = jnp.cos(angle), jnp.sin(angle)
     tail = jnp.where(lane < 96, jnp.where(run > lane - 64, -BIG, 0.0), 0.0)
-    loads[3].wait()
-    loads[4].wait()
     for i in range(4):
         uk_t[:, 128 * i : 128 * i + 128] = uk_ref[i].T
         up_t[128 * i : 128 * i + 128, :] = up_ref[i].T
@@ -151,7 +158,7 @@
     rope = jnp.where(lane < 64, rope * cosine + swapped * sine, tail)
     near_ref[core, 0, p, q, :, 512:] = rope.astype(BF16)
     block = near_ref.at[core, 0, p, q]
-    p_z = [copy(block, far_ref.at[core, p, q, d - 2], zs[d]) for d in range(2, 7)]
+    p_z = [copy(block, far_ref.at[core, p, q, d - 2], zs[d]) for d in (2, 6, 3, 5, 4)]
     p_p = [copy(block, block, who) for who in plane]
 
     for c in p_q:
@@ -166,12 +173,6 @@
 
     def share(part):
         return copy(part, part, sibling)
-
-    for c in p_p:
-        c.wait()
-    mine = near_ref.at[core, 0]
-    beside = [copy(mine, near_ref.at[core, 1], zs[1]), copy(mine, near_ref.at[core, 2], zs[7])]
-    s_near = [share(mine)]
 
     for c in p_z:
         c.wait()
@@ -190,6 +191,12 @@
     lines = {0: spread(0, across)}
     s_lines = {}
 
+    for c in p_p:
+        c.wait()
+    mine = near_ref.at[core, 0]
+    beside = [copy(mine, near_ref.at[core, 1], zs[1]), copy(mine, near_ref.at[core, 2], zs[7])]
+    s_near = [share(mine)]
+
     def finish(a):
         for c in lines[a]:
             c.wait()
@@ -210,16 +217,16 @@
     def expand(n, keys, which):
         keys = keys(which, slice(0, 512))
         count = keys.shape[0]
-        ke[n, :count] = dot(keys, uk_t[...]).astype(BF16)
+        ke[n, :count] = (dot(keys, uk_t[...]) * scale).astype(BF16)
         vt[n, :, :count] = dot(up_t[...], keys, 1, 1).astype(BF16)
 
-    def attend(n, keys, which, diagonal=False):
+    def score(n, keys, which, i, diagonal=False):
         tails = keys(which, slice(512, KW))
         count = tails.shape[0]
-        for i in range(4):
-            s_ref[i, :count] = dot(jnp.concatenate([ke[n, :count, 128 * i : 128 * i + 128], tails], 1), qt[i])
+        s_ref[n % 2, i, :count] = dot(jnp.concatenate([ke[n, :count, 128 * i : 128 * i + 128], tails], 1), qt[i])
         if diagonal:
-            token = lax.broadcasted_iota(jnp.int32, (16, 256), 1)
+            at = lax.broadcasted_iota(jnp.int32, (16, 256), 1)
+            token = at % 128 // 16 * 32 + at // 128 * 16 + at % 16
             row = lax.broadcasted_iota(jnp.int32, (16, 256), 0)
             for k in range(2):
                 for ky in range(4):
@@ -228,74 +235,90 @@
                         strip = pl.ds(pl.multiple_of(k * 256 + at * 16, 16), 16)
                         key_token = (ky * 4 + half * 2 + k) * 16 + row
                         hidden = (key_token > token) & (key_token // 128 == token // 128)
-                        for i in range(4):
-                            s_ref[i, strip] = jnp.where(hidden, -BIG, s_ref[i, strip])
+                        s_ref[n % 2, i, strip] = jnp.where(hidden, -BIG, s_ref[n % 2, i, strip])
+
+    def weigh(n, count, i):
+        s = s_ref[n % 2, i, :count]
+        before = m[i]
+        now = jnp.maximum(before, jnp.max(s, 0, keepdims=True))
+        w = jnp.exp2(s - now)
+        fade = jnp.exp2(before - now)
+        l[i] = l[i] * fade + jnp.sum(w, 0, keepdims=True)
+        m[i] = now
+        acc[i] = acc[i] * fade + dot(vt[n, 128 * i : 128 * i + 128, :count], w.astype(BF16))
+
+    def step(n, count, keys, which):
         for i in range(4):
-            s = s_ref[i, :count] * scale
-            before = m[i]
-            now = jnp.maximum(before, jnp.max(s, 0, keepdims=True))
-            w = jnp.exp2(s - now)
-            fade = jnp.exp2(before - now)
-            l[i] = l[i] * fade + jnp.sum(w, 0, keepdims=True)
-            m[i] = now
-            acc[i] = acc[i] * fade + dot(vt[n, 128 * i : 128 * i + 128, :count], w.astype(BF16))
+            score(n, keys, which, i)
+            weigh(n - 1, count, i)
 
     m[...] = jnp.full(m.shape, -4 * BIG, F32)
     l[...] = jnp.zeros(l.shape, F32)
     acc[...] = jnp.zeros(acc.shape, F32)
-    wide = lax.broadcasted_iota(jnp.int32, (32, 256), 1)
-    base = jnp.where(wide < 128, pos_ref[0], pos_ref[128])
-    angle = (base + wide % 128).astype(F32) * inv_col_ref[...]
-    cosine, sine = jnp.cos(angle), jnp.sin(angle)
-    runs = jnp.where(base // 128 == lax.broadcasted_iota(jnp.int32, (32, 256), 0), 1.0, 0.0).astype(BF16)
+
+    def queries(k):
+        wide = lax.broadcasted_iota(jnp.int32, (32, 128), 1)
+        base = jnp.where(wide < 64, pos_ref[0], pos_ref[128])
+        angle = (base + wide % 64 // 16 * 32 + k * 16 + wide % 16).astype(F32) * inv_col_ref[...]
+        cosine, sine = jnp.cos(angle), jnp.sin(angle)
+        runs = jnp.where(base // 128 == lax.broadcasted_iota(jnp.int32, (32, 128), 0), 1.0, 0.0).astype(BF16)
+        at = pl.ds(pl.multiple_of(k * 128, 128), 128)
+        q_t = dot(cq_ref[:, pl.ds(k, 1)].reshape(128, 1536), wqb_ref[...]).astype(BF16).T
+        for i in range(4):
+            qt[i, :128, at] = q_t[192 * i : 192 * i + 128]
+            a = q_t[192 * i + 128 : 192 * i + 160].astype(F32)
+            b = q_t[192 * i + 160 : 192 * i + 192].astype(F32)
+            qt[i, 128:160, at] = ((a * cosine - b * sine) * scale).astype(BF16)
+            qt[i, 160:192, at] = ((b * cosine + a * sine) * scale).astype(BF16)
+            qt[i, 192:224, at] = runs
+            qt[i, 224:, at] = jnp.zeros((32, 128), BF16)
+
     s_near[0].wait()
     expand(0, near_keys, 0)
     for c in p_c:
         c.wait()
     mate = cq_ref.at[:, pl.ds(core, 1)]
     c_c = share(mate)
-    for c, a in zip(first, (3, 1, 2)):
-        c.wait()
+    for n, a in ((0, 3), (1, 1), (2, 2)):
+        first[n].wait()
         lines[a] = spread(a, across)
-    loads[5].wait()
+    loads[9].wait()
+    queries(core)
     c_c.wait()
-    q_t = dot(cq_ref[...].reshape(256, 1536), wqb_ref[...]).astype(BF16).T
+    queries(1 - core)
+    finish(0)
     for i in range(4):
-        qt[i, :128] = q_t[192 * i : 192 * i + 128]
-        a = q_t[192 * i + 128 : 192 * i + 160].astype(F32)
-        b = q_t[192 * i + 160 : 192 * i + 192].astype(F32)
-        qt[i, 128:160] = (a * cosine - b * sine).astype(BF16)
-        qt[i, 160:192] = (b * cosine + a * sine).astype(BF16)
-        qt[i, 192:224] = runs
-        qt[i, 224:] = jnp.zeros((32, 256), BF16)
-    finish(0)
-    attend(0, near_keys, 0, True)
+        score(0, near_keys, 0, i, True)
     for r in (1, 2):
         beside[r - 1].wait()
         s_near.append(share(near_ref.at[core, r]))
     s_lines[0].wait()
-    expand(3, far_keys, 0)
+    expand(1, far_keys, 0)
+    step(1, 512, far_keys, 0)
     finish(3)
-    attend(3, far_keys, 0)
     s_near[1].wait()
-    expand(1, near_keys, 1)
-    attend(1, near_keys, 1)
+    expand(2, near_keys, 1)
+    step(2, 640, near_keys, 1)
+    s_near[2].wait()
+    expand(3, near_keys, 2)
+    step(3, 512, near_keys, 2)
     finish(1)
     s_lines[3].wait()
     expand(4, far_keys, 3)
-    attend(4, far_keys, 3)
-    s_near[2].wait()
-    expand(2, near_keys, 2)
-    attend(2, near_keys, 2)
-    finish(2)
+    step(4, 512, far_keys, 3)
     s_lines[1].wait()
     expand(5, far_keys, 1)
-    attend(5, far_keys, 1)
+    finish(2)
+    step(5, 640, far_keys, 1)
     s_lines[2].wait()
     expand(6, far_keys, 2)
-    attend(6, far_keys, 2)
+    step(6, 640, far_keys, 2)
     for i in range(4):
-        out_ref[:, 128 * i : 128 * i + 128] = (acc[i] / l[i]).T.astype(BF16)
+        weigh(6, 640, i)
+    for i in range(4):
+        values = (acc[i] / l[i]).T.astype(BF16)
+        for k in range(2):
+            out_ref[:, k, :, 128 * i : 128 * i + 128] = values[128 * k : 128 * k + 128].reshape(8, 16, 128)
 
 
 def body(hidden_in, w_qa, w_kva, q_norm_gain, kv_norm_gain, w_qb, w_uk, value_up_weight, positions):
@@ -303,7 +326,7 @@
     inv_row = np.zeros((1, 128), np.float32)
     inv_row[0, :32] = inverse
     inv_row[0, 32:64] = inverse
-    inv_col = np.repeat(inverse.astype(np.float32)[:, None], 256, 1)
+    inv_col = np.repeat(inverse.astype(np.float32)[:, None], 128, 1)
     vmem = pl.BlockSpec(memory_space=pltpu.VMEM)
     smem = pl.BlockSpec(memory_space=pltpu.SMEM)
     any_space = pl.BlockSpec(memory_space=pl.ANY)
@@ -311,10 +334,11 @@
     return pl.pallas_call(
         kernel,
         name="attention",
-        out_shape=jax.ShapeDtypeStruct((256, 512), BF16),
-        in_specs=[smem] + [vmem] * 4 + [any_space] * 6,
+        out_shape=jax.ShapeDtypeStruct((8, 2, 16, 512), BF16),
+        in_specs=[smem] + [any_space] * 10,
         out_specs=vmem,
         scratch_shapes=[
+            pltpu.VMEM((1, 128), F32), pltpu.VMEM((32, 128), F32), pltpu.VMEM((1536,), F32), pltpu.VMEM((512,), F32),
             pltpu.VMEM((448, 256), BF16), pltpu.VMEM((448, 1536), BF16), pltpu.VMEM((448, 576), BF16),
             pltpu.VMEM((1536, 768), BF16), pltpu.VMEM((4, 128, 512), BF16), pltpu.VMEM((4, 512, 128), BF16),
             pltpu.VMEM((2, 128, 448), BF16), pltpu.VMEM((512, 512), BF16), pltpu.VMEM((512, 512), BF16),
@@ -326,9 +350,9 @@
             pltpu.VMEM((8, 2, 16, 1536), BF16), pltpu.VMEM((2, 3, 4, 4, 16, KW), BF16),
             pltpu.VMEM((2, 4, 4, 5, 16, KW), BF16),
             pltpu.VMEM((7, 640, 512), BF16), pltpu.VMEM((7, 512, 640), BF16),
-            pltpu.VMEM((4, 256, 256), BF16), pltpu.VMEM((4, 640, 256), F32),
+            pltpu.VMEM((4, 256, 256), BF16), pltpu.VMEM((2, 4, 640, 256), F32),
             pltpu.VMEM((4, 128, 256), F32), pltpu.VMEM((4, 1, 256), F32), pltpu.VMEM((4, 1, 256), F32),
-            pltpu.SemaphoreType.DMA((copies,)), pltpu.SemaphoreType.DMA((copies,)), pltpu.SemaphoreType.DMA((6,)),
+            pltpu.SemaphoreType.DMA((copies,)), pltpu.SemaphoreType.DMA((copies,)), pltpu.SemaphoreType.DMA((10,)),
         ],
         compiler_params=pltpu.CompilerParams(
             collective_id=0, has_side_effects=True, vmem_limit_bytes=60 * 2**20
@@ -336,7 +360,7 @@
     )(
         positions, jnp.asarray(inv_row), jnp.asarray(inv_col), q_norm_gain, kv_norm_gain,
         hidden_in.T, w_qa, w_kva, w_qb, w_uk, value_up_weight,
-    )
+    ).reshape(256, 512)
 
 
 def solution(mesh):

time: 52.1 us -> 52.8 us (1.013)
  Pallas kernels: 50.2 us -> 50.9 us
    pallas_call x1, Pallas kernels: 50.2 us -> 50.9 us  [body(): pl.pallas_call(kernel, name='attention', out_shape=jax.ShapeDtypeStruct((...]
where the time goes in v3:
time: 52.8 us; the launch traced here: 52.6 us
  Pallas kernels  50.9 us (96%)
  local copies, waits for them, and re-layouts  1.67 us (3%)
    pallas_call x1, Pallas kernels, body(): pl.pallas_call(kernel, name='attention', out_shape=jax.ShapeDtypeStruct((...  50.9 us
    unnamed x1, local copies, waits for them, and re-layouts  1.67 us

profile of v3, /device:TPU:1, one launch (start us, length us, event | category | flops | bytes accessed | tf_op | source)
XLA Modules:
  0.0 52.6 jit_solution(16728046983570949091)
XLA Ops:
  0.0 50.9 %attention.1 = bf16[8,2,16,512]{3,2,1,0:T(8,128)(2,1)} custom-call(s32[256]{0:T(256)} %pos_ref.1, f32[1,128]{1,0:T(1,128)} %constant.4.clone.row_hbm, f32[32,128]{1,0:T(8,128)} %constant.5.clone.col_hbm, f32[1536]{0:T(1024)} %qg_hbm.1, f32[512]{0:T(512)} %kg_hbm.1, bf16[448,256]{1,0:T(8,128)(2,1)} %bitcast.3, bf16[448,1536]{1,0:T(8,128)(2,1)} %wqa_hbm.1, ...), custom_call_target="tpu_custom_call" | custom-call | tf_op jit(solution)/shard_map/attention/pallas_call | solution.py:334
  50.9 1.7 %copy.13 = bf16[256,512]{1,0:T(8,128)(2,1)} copy(bf16[256,512]{1,0:T(8,128)(2,1)} %bitcast.2) | data formatting | bytes 524288

commit v4 on v3

--- a/solution.py
+++ b/solution.py
@@ -334,7 +334,7 @@
     return pl.pallas_call(
         kernel,
         name="attention",
-        out_shape=jax.ShapeDtypeStruct((8, 2, 16, 512), BF16),
+        out_shape=pltpu.VMEM((8, 2, 16, 512), BF16),
         in_specs=[smem] + [any_space] * 10,
         out_specs=vmem,
         scratch_shapes=[

time: 52.8 us -> 51.1 us (0.968)
  local copies, waits for them, and re-layouts: 1.67 us -> 0.71 us
  Pallas kernels: 50.9 us -> 50.2 us
    unnamed x1, local copies, waits for them, and re-layouts: 1.67 us -> 0.71 us
    pallas_call x1, Pallas kernels: 50.9 us -> 50.2 us  [body(): pl.pallas_call(kernel, name='attention', out_shape=pltpu.VMEM((8, 2, 16,...]
where the time goes in v4:
time: 51.1 us; the launch traced here: 50.9 us
  Pallas kernels  50.2 us (98%)
  local copies, waits for them, and re-layouts  0.71 us (1%)
    pallas_call x1, Pallas kernels, body(): pl.pallas_call(kernel, name='attention', out_shape=pltpu.VMEM((8, 2, 16,...  50.2 us

profile of v4, /device:TPU:1, one launch (start us, length us, event | category | flops | bytes accessed | tf_op | source)
XLA Modules:
  0.0 50.9 jit_solution(7545280858629370016)
XLA Ops:
  0.0 50.2 %attention.1 = bf16[8,2,16,512]{3,2,1,0:T(8,128)(2,1)S(1)} custom-call(s32[256]{0:T(256)} %pos_ref.1, f32[1,128]{1,0:T(1,128)} %constant.4.clone.row_hbm, f32[32,128]{1,0:T(8,128)} %constant.5.clone.col_hbm, f32[1536]{0:T(1024)} %qg_hbm.1, f32[512]{0:T(512)} %kg_hbm.1, bf16[448,256]{1,0:T(8,128)(2,1)} %bitcast.3, bf16[448,1536]{1,0:T(8,128)(2,1)} %wqa_hbm.1, ...), custom_call_target="tpu_custom_call" | custom-call | tf_op jit(solution)/shard_map/attention/pallas_call | solution.py:334
  50.2 0.7 %copy.13 = bf16[256,512]{1,0:T(8,128)(2,1)} copy(bf16[256,512]{1,0:T(8,128)(2,1)S(1)} %bitcast.2) | data formatting | bytes 524288

commit v5 on v4

--- a/solution.py
+++ b/solution.py
@@ -81,11 +81,11 @@
 
     sibling = device(1 - core, x, y, z)
     peers = []
-    for dy, dx in ((2, 1), (1, 1), (3, 1), (2, 0), (0, 1), (1, 0), (3, 0)):
+    for dy, dx in ((0, 1), (1, 0), (1, 1), (2, 0), (2, 1), (3, 0), (3, 1)):
         py, px = (y + dy) % 4, (xh + dx) % 2
         peers.append((py * 2 + px, device(core, px * 2 + xl, py, z)))
     zs = [device(core, x, y, (z + d) % 8) for d in range(8)]
-    order = (10, 9, 11, 6, 14, 2, 8, 5, 7, 13, 15, 1, 3, 4, 12)
+    order = range(1, 16)
     plane = [device(core, (x + d % 4) % 4, (y + d // 4) % 4, z) for d in order]
     barrier = pltpu.get_barrier_semaphore()
     greet = [sibling] + zs[1:] + plane
@@ -284,14 +284,14 @@
         lines[a] = spread(a, across)
     loads[9].wait()
     queries(core)
+    finish(0)
     c_c.wait()
     queries(1 - core)
-    finish(0)
-    for i in range(4):
-        score(0, near_keys, 0, i, True)
     for r in (1, 2):
         beside[r - 1].wait()
         s_near.append(share(near_ref.at[core, r]))
+    for i in range(4):
+        score(0, near_keys, 0, i, True)
     s_lines[0].wait()
     expand(1, far_keys, 0)
     step(1, 512, far_keys, 0)

time: 51.1 us -> 49.3 us (0.965)
  Pallas kernels: 50.2 us -> 48.5 us
    pallas_call x1, Pallas kernels: 50.2 us -> 48.5 us  [body(): pl.pallas_call(kernel, name='attention', out_shape=pltpu.VMEM((8, 2, 16,...]
where the time goes in v5:
time: 49.3 us; the launch traced here: 49.2 us
  Pallas kernels  48.5 us (98%)
  local copies, waits for them, and re-layouts  0.71 us (1%)
    pallas_call x1, Pallas kernels, body(): pl.pallas_call(kernel, name='attention', out_shape=pltpu.VMEM((8, 2, 16,...  48.5 us

profile of v5, /device:TPU:1, one launch (start us, length us, event | category | flops | bytes accessed | tf_op | source)
XLA Modules:
  0.0 49.2 jit_solution(5852326554767597033)
XLA Ops:
  0.0 48.5 %attention.1 = bf16[8,2,16,512]{3,2,1,0:T(8,128)(2,1)S(1)} custom-call(s32[256]{0:T(256)} %pos_ref.1, f32[1,128]{1,0:T(1,128)} %constant.4.clone.row_hbm, f32[32,128]{1,0:T(8,128)} %constant.5.clone.col_hbm, f32[1536]{0:T(1024)} %qg_hbm.1, f32[512]{0:T(512)} %kg_hbm.1, bf16[448,256]{1,0:T(8,128)(2,1)} %bitcast.3, bf16[448,1536]{1,0:T(8,128)(2,1)} %wqa_hbm.1, ...), custom_call_target="tpu_custom_call" | custom-call | tf_op jit(solution)/shard_map/attention/pallas_call | solution.py:334
  48.5 0.7 %copy.13 = bf16[256,512]{1,0:T(8,128)(2,1)} copy(bf16[256,512]{1,0:T(8,128)(2,1)S(1)} %bitcast.2) | data formatting | bytes 524288

commit v6 on v5

--- a/solution.py
+++ b/solution.py
@@ -202,6 +202,12 @@
             c.wait()
         s_lines[a] = share(far_ref.at[core, (p + a) % 4])
 
+    def finish_last(a):
+        s_lines[a] = [share(far_ref.at[core, (p + a) % 4, q])]
+        for c, b in zip(lines[a], (3, 1, 2)):
+            c.wait()
+            s_lines[a].append(share(far_ref.at[core, (p + a) % 4, (q + b) % 4]))
+
     sp = y * (1 - core) + x * core
     scale = math.log2(math.e) / math.sqrt(192)
 
@@ -308,11 +314,15 @@
     step(4, 512, far_keys, 3)
     s_lines[1].wait()
     expand(5, far_keys, 1)
-    finish(2)
+    finish_last(2)
     step(5, 640, far_keys, 1)
-    s_lines[2].wait()
+    for i in range(4):
+        weigh(5, 640, i)
+    for c in s_lines[2]:
+        c.wait()
     expand(6, far_keys, 2)
-    step(6, 640, far_keys, 2)
+    for i in range(4):
+        score(6, far_keys, 2, i)
     for i in range(4):
         weigh(6, 640, i)
     for i in range(4):

time: 49.3 us -> 49.1 us (level)
  no operation moved by 1% of the time
where the time goes in v6:
time: 49.1 us; the launch traced here: 48.9 us
  Pallas kernels  48.2 us (98%)
  local copies, waits for them, and re-layouts  0.71 us (1%)
    pallas_call x1, Pallas kernels, body(): pl.pallas_call(kernel, name='attention', out_shape=pltpu.VMEM((8, 2, 16,...  48.2 us

profile of v6, /device:TPU:1, one launch (start us, length us, event | category | flops | bytes accessed | tf_op | source)
XLA Modules:
  0.0 48.9 jit_solution(5635315050655541218)
XLA Ops:
  0.0 48.2 %attention.1 = bf16[8,2,16,512]{3,2,1,0:T(8,128)(2,1)S(1)} custom-call(s32[256]{0:T(256)} %pos_ref.1, f32[1,128]{1,0:T(1,128)} %constant.4.clone.row_hbm, f32[32,128]{1,0:T(8,128)} %constant.5.clone.col_hbm, f32[1536]{0:T(1024)} %qg_hbm.1, f32[512]{0:T(512)} %kg_hbm.1, bf16[448,256]{1,0:T(8,128)(2,1)} %bitcast.3, bf16[448,1536]{1,0:T(8,128)(2,1)} %wqa_hbm.1, ...), custom_call_target="tpu_custom_call" | custom-call | tf_op jit(solution)/shard_map/attention/pallas_call | solution.py:344
  48.2 0.7 %copy.13 = bf16[256,512]{1,0:T(8,128)(2,1)} copy(bf16[256,512]{1,0:T(8,128)(2,1)S(1)} %bitcast.2) | data formatting | bytes 524288
